TPU v7x, 32 devices: a whole 2x2x4 slice. The times are simulated.
32 devices in a mesh: dp: 8 (over z, x), seq: 4 (over y, core).
Axes of the slice: x: 2, y: 2, z: 4, core: 2. Of those that a mesh axis runs over, the one named last changes fastest.
Arguments:
- tokens: bfloat16 [8, 512, 1024], P('dp', 'seq'), may hold values from -6 to 6
- cotangent: bfloat16 [8, 512, 2048], P('dp', 'seq'), may hold values from -6 to 6
- input_weight: bfloat16 [1024, 4096], P('dp'), may hold values from -0.1875 to 0.1875
- filter_weight: float32 [2, 4, 2048], P(None, None, 'dp'), may hold values from -3 to 3
- filter_bias: float32 [2, 2048], P(None, 'dp'), may hold values from -0.5 to 0.5
- scan_weight: float32 [2, 2048, 96], P(None, 'dp'), may hold values from -0.125 to 0.125
- step_weight: float32 [2, 64, 2048], P(None, None, 'dp'), may hold values from -0.75 to 0.75
- step_bias: float32 [2, 2048], P(None, 'dp'), may hold values from -6 to -2.5
- log_rate: float32 [2, 16, 2048], P(None, None, 'dp'), may hold values from -4 to 1
- skip_gain: float32 [2, 2048], P(None, 'dp'), may hold values from 0.5 to 1.5
Outputs:
- mixed: bfloat16 [8, 512, 2048], P('dp', 'seq')
- tokens_gradient: bfloat16 [8, 512, 1024], P('dp', 'seq')
- input_weight_gradient: float32 [1024, 4096], P(('dp', 'seq'))
- filter_weight_gradient: float32 [2, 4, 2048], P(None, None, ('dp', 'seq'))
- filter_bias_gradient: float32 [2, 2048], P(None, ('dp', 'seq'))
- scan_weight_gradient: float32 [2, 2048, 96], P(None, ('dp', 'seq'))
- step_weight_gradient: float32 [2, 64, 2048], P(None, None, ('dp', 'seq'))
- step_bias_gradient: float32 [2, 2048], P(None, ('dp', 'seq'))
- log_rate_gradient: float32 [2, 16, 2048], P(None, None, ('dp', 'seq'))
- skip_gain_gradient: float32 [2, 2048], P(None, ('dp', 'seq'))
All inputs are finite; a program needn't handle non-finite values.
Results may differ from a plain program's by a relative error of at most 0.0072.
Values may be sent and summed in bfloat16 or wider, within the bound.
A program may use at most 128 MiB of HBM per device.

v0:
```python
from functools import partial

import jax
import jax.numpy as jnp
from jax import lax
from jax.sharding import PartitionSpec as P

N = 16
K = 4
R = 64
BLOCK = 8


HIGH = lax.Precision.HIGHEST


def prefix(part, axis, combine, identity, reverse):
    count = lax.axis_size(axis)
    place = lax.axis_index(axis)
    ahead = count - 1 - place if reverse else place
    gathered = jax.tree.map(lambda a: lax.all_gather(a, axis), part)
    state = jax.tree.map(lambda a, e: jnp.zeros_like(a) + jnp.asarray(e, a.dtype), part, identity)

    def one(step, state):
        source = count - 1 - step if reverse else step
        return combine(
            state, jax.tree.map(lambda a: lax.dynamic_index_in_dim(a, source, 0, False), gathered)
        )

    return lax.fori_loop(0, ahead, one, state)


def extended(x, sides, width):
    for axis, dim in sides:
        peers, length = (lax.axis_size(axis), x.shape[dim])
        up = [(i, (i + 1) % peers) for i in range(peers - 1)]
        down = [(j, i) for i, j in up]
        last = lax.slice_in_dim(x, length - width, length, axis=dim)
        first = lax.slice_in_dim(x, 0, width, axis=dim)
        before = lax.ppermute(last, axis, up)
        after = lax.ppermute(first, axis, down)
        x = jnp.concatenate([before, x, after], axis=dim)
    return x


def combine_pair(earlier, later):
    return (earlier[0] * later[0], later[0] * earlier[1] + later[1])


def block_scan(state_in, active, steps, inputs, reads, log_rate, skip_gain):
    rate = -jnp.exp(log_rate)
    length = active.shape[0]
    count = length // BLOCK

    def block_advance(state, block):
        active_part, step_part, input_part, read_part = block
        drive_part = step_part * active_part
        results = []
        for place in range(BLOCK):
            state = (
                jnp.exp(step_part[place][None] * rate) * state
                + drive_part[place][None] * input_part[place][:, None]
            )
            results.append(jnp.dot(read_part[place], state, precision=HIGH))
        result = jnp.stack(results) + skip_gain * active_part
        return (state, result)

    blocks = tuple(
        (array.reshape(count, BLOCK, array.shape[1]) for array in (active, steps, inputs, reads))
    )
    state_out, results = lax.scan(jax.checkpoint(block_advance), state_in, blocks)
    return (results.reshape(length, active.shape[1]), state_out)


def prepare(padded, filter_weight, filter_bias, scan_weight, step_weight, step_bias, which):
    length = padded.shape[0] - 2 * (K - 1)
    filtered = filter_bias[which]
    for tap in range(K):
        start = tap if which == 0 else 2 * (K - 1) - tap
        filtered = filtered + filter_weight[which, tap] * padded[start : start + length]
    active = jax.nn.silu(filtered)
    coefficients = jnp.dot(active, scan_weight[which], precision=HIGH)
    steps = jax.nn.softplus(
        jnp.dot(coefficients[:, :R], step_weight[which], precision=HIGH) + step_bias[which]
    )
    return (active, steps, coefficients[:, R : R + N], coefficients[:, R + N :])


def forward_summary(active, steps, inputs, log_rate):
    rate = -jnp.exp(log_rate)
    count = active.shape[0] // BLOCK

    def forward_advance(carry, block):
        state, elapsed = carry
        active_part, step_part, input_part = block
        within = jnp.cumsum(step_part, axis=0)
        span = within[-1]
        weights = (
            jnp.exp((span[None] - within)[:, None, :] * rate[None])
            * (step_part * active_part)[:, None, :]
        )
        local = jnp.einsum("qn,qne->ne", input_part, weights, precision=HIGH)
        return ((jnp.exp(span[None] * rate) * state + local, elapsed + span), None)

    blocks = tuple(
        (array.reshape(count, BLOCK, array.shape[1]) for array in (active, steps, inputs))
    )
    start = (jnp.zeros(rate.shape, jnp.float32), jnp.zeros(rate.shape[1:], jnp.float32))
    (state, elapsed), _ = lax.scan(forward_advance, start, blocks)
    return (jnp.exp(elapsed[None] * rate), state)


def adjoint_summary(steps, reads, back_out, log_rate):
    rate = -jnp.exp(log_rate)
    count = steps.shape[0] // BLOCK

    def adjoint_advance(elapsed, block):
        step_part, read_part, back_part = block
        within = elapsed[None] + jnp.cumsum(step_part, axis=0)
        weights = jnp.exp(within[:, None, :] * rate[None]) * back_part[:, None, :]
        return (within[-1], jnp.einsum("qn,qne->ne", read_part, weights, precision=HIGH))

    blocks = tuple(
        (array.reshape(count, BLOCK, array.shape[1]) for array in (steps, reads, back_out))
    )
    _, parts = lax.scan(adjoint_advance, jnp.zeros(steps.shape[1:], jnp.float32), blocks)
    return jnp.sum(parts, axis=0)


def pass_states(rising, falling):
    rise_start = (jnp.ones_like(rising[0]), jnp.zeros_like(rising[1]))
    below = prefix(rising, "seq", combine_pair, rise_start, False)
    fall_start = (jnp.ones_like(falling[0]), jnp.zeros_like(falling[1]))
    above = prefix(falling, "seq", combine_pair, fall_start, True)
    return (below[1], above[1])


def shards(
    tokens,
    cotangent,
    input_weight,
    filter_weight,
    filter_bias,
    scan_weight,
    step_weight,
    step_bias,
    log_rate,
    skip_gain,
):
    full_weight = lax.all_gather(input_weight, "dp", axis=0, tiled=True)
    params = (
        lax.all_gather(filter_weight, "dp", axis=2, tiled=True),
        lax.all_gather(filter_bias, "dp", axis=1, tiled=True),
        lax.all_gather(scan_weight, "dp", axis=1, tiled=True),
        lax.all_gather(step_weight, "dp", axis=2, tiled=True),
        lax.all_gather(step_bias, "dp", axis=1, tiled=True),
        lax.all_gather(log_rate, "dp", axis=2, tiled=True),
        lax.all_gather(skip_gain, "dp", axis=1, tiled=True),
    )
    inputs = tokens[0]
    projected = jnp.dot(inputs, full_weight, preferred_element_type=jnp.float32).astype(
        jnp.bfloat16
    )
    width = projected.shape[1] // 2
    rim = K - 1
    widened = extended(projected[:, :width], (("seq", 0),), rim)
    padded = widened.astype(jnp.float32)
    gates = projected[:, width:].astype(jnp.float32)
    prepared_list = []
    prep_pulls = []
    summaries = []
    for which in range(2):
        prepared, prep_pull = jax.vjp(
            partial(prepare, which=which),
            padded,
            params[0],
            params[1],
            params[2],
            params[3],
            params[4],
        )
        if which == 1:
            prepared = tuple((array[::-1] for array in prepared))
        prepared_list.append(prepared)
        prep_pulls.append(prep_pull)
        summaries.append(forward_summary(prepared[0], prepared[1], prepared[2], params[5][which]))
    start_rise, start_fall = pass_states(summaries[0], summaries[1])
    starts = (start_rise, start_fall)
    outputs = []
    scan_pulls = []
    for which in range(2):
        active, steps, inputs_coef, reads = prepared_list[which]
        result, scan_pull = jax.vjp(
            block_scan,
            starts[which],
            active,
            steps,
            inputs_coef,
            reads,
            params[5][which],
            params[6][which],
        )
        outputs.append(result[0])
        scan_pulls.append(scan_pull)
    total = outputs[0] + outputs[1][::-1]
    gate, gate_pull = jax.vjp(jax.nn.silu, gates)
    mixed = (total * gate).astype(jnp.bfloat16)
    tangent = cotangent[0].astype(jnp.float32)
    back_total = tangent * gate
    back_gates = gate_pull(tangent * total)[0]
    directed = (back_total, back_total[::-1])
    flows = []
    for which in range(2):
        flows.append(
            adjoint_summary(
                prepared_list[which][1], prepared_list[which][3], directed[which], params[5][which]
            )
        )
    late_one, late_zero = pass_states((summaries[1][0], flows[1]), (summaries[0][0], flows[0]))
    lates = (late_zero, late_one)
    back_padded = jnp.zeros_like(padded)
    param_backs = [jnp.zeros_like(param) for param in params[:5]]
    rate_rows = []
    skip_rows = []
    for which in range(2):
        backs = scan_pulls[which]((directed[which], lates[which]))
        prep_backs = backs[1:5]
        if which == 1:
            prep_backs = tuple((array[::-1] for array in prep_backs))
        more = prep_pulls[which](prep_backs)
        back_padded = back_padded + more[0]
        param_backs = [older + newer for older, newer in zip(param_backs, more[1:])]
        rate_rows.append(backs[5])
        skip_rows.append(backs[6])
    packed = jnp.concatenate([back_padded[:rim], back_padded[-rim:]], axis=0)
    returned = extended(packed, (("seq", 0),), rim)
    middle = back_padded[rim:-rim]
    back_values = jnp.concatenate(
        [middle[:rim] + returned[:rim], middle[rim:-rim], middle[-rim:] + returned[-rim:]], axis=0
    )
    back_projected = jnp.concatenate([back_values, back_gates], axis=1).astype(jnp.bfloat16)
    tokens_back = lax.dot_general(
        back_projected, full_weight, (((1,), (1,)), ((), ())), preferred_element_type=jnp.float32
    ).astype(jnp.bfloat16)
    weight_back = lax.dot_general(
        inputs, back_projected, (((0,), (0,)), ((), ())), preferred_element_type=jnp.float32
    )
    rates_back = jnp.stack(rate_rows)
    skip_back = jnp.stack(skip_rows)
    group_sums = (
        lax.psum_scatter(weight_back, "dp", scatter_dimension=0, tiled=True),
        lax.psum_scatter(param_backs[0], "dp", scatter_dimension=2, tiled=True),
        lax.psum_scatter(param_backs[1], "dp", scatter_dimension=1, tiled=True),
        lax.psum_scatter(param_backs[2], "dp", scatter_dimension=1, tiled=True),
        lax.psum_scatter(param_backs[3], "dp", scatter_dimension=2, tiled=True),
        lax.psum_scatter(param_backs[4], "dp", scatter_dimension=1, tiled=True),
        lax.psum_scatter(rates_back, "dp", scatter_dimension=2, tiled=True),
        lax.psum_scatter(skip_back, "dp", scatter_dimension=1, tiled=True),
    )
    sums = (
        lax.psum_scatter(group_sums[0], "seq", scatter_dimension=0, tiled=True),
        lax.psum_scatter(group_sums[1], "seq", scatter_dimension=2, tiled=True),
        lax.psum_scatter(group_sums[2], "seq", scatter_dimension=1, tiled=True),
        lax.psum_scatter(group_sums[3], "seq", scatter_dimension=1, tiled=True),
        lax.psum_scatter(group_sums[4], "seq", scatter_dimension=2, tiled=True),
        lax.psum_scatter(group_sums[5], "seq", scatter_dimension=1, tiled=True),
        lax.psum_scatter(group_sums[6], "seq", scatter_dimension=2, tiled=True),
        lax.psum_scatter(group_sums[7], "seq", scatter_dimension=1, tiled=True),
    )
    return (
        mixed[None],
        tokens_back[None],
        sums[0],
        sums[1],
        sums[2],
        sums[3],
        sums[4],
        sums[5],
        sums[6],
        sums[7],
    )


def solution(mesh):
    in_specs = (
        P("dp", "seq", None),
        P("dp", "seq", None),
        P("dp", None),
        P(None, None, "dp"),
        P(None, "dp"),
        P(None, "dp", None),
        P(None, None, "dp"),
        P(None, "dp"),
        P(None, None, "dp"),
        P(None, "dp"),
    )
    out_specs = (
        P("dp", "seq", None),
        P("dp", "seq", None),
        P(("dp", "seq"), None),
        P(None, None, ("dp", "seq")),
        P(None, ("dp", "seq")),
        P(None, ("dp", "seq"), None),
        P(None, None, ("dp", "seq")),
        P(None, ("dp", "seq")),
        P(None, None, ("dp", "seq")),
        P(None, ("dp", "seq")),
    )
    return jax.shard_map(shards, mesh=mesh, in_specs=in_specs, out_specs=out_specs, check_vma=False)
```

profile of v0, /device:TPU:0, one launch (start us, length us, event | category | flops | bytes accessed | tf_op | source)
XLA Modules:
  0.0 2150.1 jit_solution(11975823674615246131)
XLA Ops:
  9.5 32.8 %all_gather.61 = f32[2,4,2048]{2,1,0:T(4,128)S(1)} all-gather(f32[2,4,256]{2,1,0:T(4,128)} %param.38), channel_id=1, replica_groups=mesh['dp'=8,'seq'=4] {'dp'}, dimensions={2}, use_global_device_ids=true | all-gather | bytes 73728 | tf_op jit(solution)/shard_map/all_gather | solution.py:152
  42.4 26.4 %all_gather.60 = f32[2,2048]{1,0:T(2,128)S(1)} all-gather(f32[2,256]{1,0:T(2,128)} %param.39), channel_id=1, replica_groups=mesh['dp'=8,'seq'=4] {'dp'}, dimensions={1}, use_global_device_ids=true | all-gather | bytes 18432 | tf_op jit(solution)/shard_map/all_gather | solution.py:153
  68.9 26.8 %all_gather.65 = f32[2,2048]{1,0:T(2,128)S(1)} all-gather(f32[2,256]{1,0:T(2,128)} %param.42), channel_id=1, replica_groups=mesh['dp'=8,'seq'=4] {'dp'}, dimensions={1}, use_global_device_ids=true | all-gather | bytes 18432 | tf_op jit(solution)/shard_map/all_gather | solution.py:156
  95.6 32.2 %all_gather.66 = f32[2,16,2048]{2,1,0:T(8,128)S(1)} all-gather(f32[2,16,256]{2,1,0:T(8,128)} %param.43), channel_id=1, replica_groups=mesh['dp'=8,'seq'=4] {'dp'}, dimensions={2}, use_global_device_ids=true | all-gather | bytes 294912 | tf_op jit(solution)/shard_map/all_gather | solution.py:157
  127.9 26.2 %all_gather.70 = f32[2,2048]{1,0:T(2,128)S(1)} all-gather(f32[2,256]{1,0:T(2,128)S(1)} %copy-done.56), channel_id=1, replica_groups=mesh['dp'=8,'seq'=4] {'dp'}, dimensions={1}, use_global_device_ids=true | all-gather | bytes 18432 | tf_op jit(solution)/shard_map/all_gather | solution.py:158
  167.5 21.3 all-gather.10.cloned.1.call-done
  191.9 36.7 %all-gather.12.cloned.1.call-done = f32[2,64,2048]{2,1,0:T(8,128)} async-done(((f32[2,64,256]{2,1,0:T(8,128)}), f32[2,64,2048]{2,1,0:T(8,128)}) %all-gather.12.cloned.1.call-update) | async-done | bytes 1048592 | tf_op jit(solution)/shard_map/all_gather | solution.py:155
  247.1 70.3 %while.193 = (s32[]{:T(128)}, f32[16,2048]{1,0:T(8,128)S(1)}, f32[2048]{0:T(1024)S(1)}, f32[16,8,2048]{2,1,0:T(8,128)}, f32[16,2048]{1,0:T(8,128)S(1)}, /*index=...) while((s32[]{:T(128)}, f32[16,2048]{1,0:T(8,128)S(1)}, ...), condition=%wide.region_9.11_spmd.clone, body=%wide.region_7.10_spmd.clone.sunk | while | flops 3952643 | bytes 3664512 | solution.py:109
  324.7 70.3 %while.192 = (s32[]{:T(128)}, f32[16,2048]{1,0:T(8,128)S(1)}, f32[2048]{0:T(1024)S(1)}, f32[16,8,2048]{2,1,0:T(8,128)}, f32[16,2048]{1,0:T(8,128)S(1)}, /*index=...) while((s32[]{:T(128)}, f32[16,2048]{1,0:T(8,128)S(1)}, ...), condition=%wide.region_2.4_spmd.clone, body=%wide.region_0.3_spmd.clone.sunk | while | flops 3952643 | bytes 3664512 | solution.py:109
  413.2 111.1 %while.185 = (s32[]{:T(128)}, f32[16,2048]{1,0:T(8,128)S(1)}, f32[16,8,2048]{2,1,0:T(8,128)S(1)}, f32[16,16,2048]{2,1,0:T(8,128)}, f32[16,8,2048]{2,1,0:T(8,128)...) while((s32[]{:T(128)}, f32[16,2048]{1,0:T(8,128)S(1)}, ...), condition=%wide.region_6.8_spmd, body=%wide.region_5.7_spmd.sunk | while | flops 5816329 | bytes 3823917 | solution.py:71
  544.0 120.6 %while.187 = (s32[]{:T(128)}, f32[16,2048]{1,0:T(8,128)S(1)}, f32[16,8,2048]{2,1,0:T(8,128)}, f32[16,16,2048]{2,1,0:T(8,128)}, f32[16,8,2048]{2,1,0:T(8,128)}, /...) while((s32[]{:T(128)}, f32[16,2048]{1,0:T(8,128)S(1)}, ...), condition=%wide.region_13.15_spmd, body=%wide.region_12.14_spmd.sunk | while | flops 5816329 | bytes 3824425 | solution.py:71
  679.0 65.8 %while.188 = (s32[]{:T(128)}, f32[2048]{0:T(1024)S(1)}, f32[16,16,2048]{2,1,0:T(8,128)}, f32[16,8,2048]{2,1,0:T(8,128)}, f32[16,8,16]{2,1,0:T(8,128)}, /*index=5...) while((s32[]{:T(128)}, f32[2048]{0:T(1024)S(1)}, f32[16,16,2048]{2,1,0:T(8,128)}, ...), condition=%wide.region_16.18_spmd, body=%wide.region_14.17_spmd.sunk | while | flops 3801090 | bytes 3304553 | solution.py:126
  760.4 189.6 %while.194 = (s32[]{:T(128)}, f32[16,2048]{1,0:T(8,128)S(1)}, f32[2048]{0:T(1024)S(1)}, f32[16,2048]{1,0:T(8,128)S(1)}, f32[16,8,2048]{2,1,0:T(8,128)}, /*index=...) while((s32[]{:T(128)}, f32[16,2048]{1,0:T(8,128)S(1)}, ...), condition=%wide.region_46.48_spmd.clone, body=%wide.region_20.47_spmd.clone.sunk | while | flops 12701316 | bytes 8618908 | solution.py:71
  960.5 65.8 %while.190 = (s32[]{:T(128)}, f32[2048]{0:T(1024)S(1)}, f32[16,16,2048]{2,1,0:T(8,128)}, f32[16,8,2048]{2,1,0:T(8,128)}, f32[16,8,16]{2,1,0:T(8,128)}, /*index=5...) while((s32[]{:T(128)}, f32[2048]{0:T(1024)S(1)}, f32[16,16,2048]{2,1,0:T(8,128)}, ...), condition=%wide.region_49.51_spmd, body=%wide.region_47.50_spmd.sunk | while | flops 3801090 | bytes 3304553 | solution.py:126
  1036.9 159.8 %while.195 = (s32[]{:T(128)}, f32[16,2048]{1,0:T(8,128)S(1)}, f32[2048]{0:T(1024)S(1)}, f32[16,2048]{1,0:T(8,128)S(1)}, f32[16,8,2048]{2,1,0:T(8,128)}, /*index=...) while((s32[]{:T(128)}, f32[16,2048]{1,0:T(8,128)S(1)}, ...), condition=%wide.region_79.81_spmd.clone, body=%wide.region_53.80_spmd.clone.sunk | while | flops 12701316 | bytes 8625508 | solution.py:71
  1198.5 9.0 rev.39
  1215.2 8.9 rev.36
  1269.9 56.6 %reduce-scatter.58.cloned.1.call-done = f32[256,2]{1,0:T(8,128)} async-done(((f32[2048,2]{1,0:T(8,128)}), f32[256,2]{1,0:T(8,128)}) %reduce-scatter.58.cloned.1.call-update) | async-done | bytes 2064
  1326.6 65.7 %reduce-scatter.52.cloned.1.call-done = f32[256,2]{1,0:T(8,128)} async-done(((f32[2048,2]{1,0:T(8,128)}), f32[256,2]{1,0:T(8,128)}) %reduce-scatter.52.cloned.1.call-update) | async-done | bytes 2064
  1392.4 66.2 %reduce-scatter.48.cloned.1.call-done = f32[256,8]{1,0:T(8,128)} async-done(((f32[2048,8]{1,0:T(8,128)}), f32[256,8]{1,0:T(8,128)}) %reduce-scatter.48.cloned.1.call-update) | async-done | bytes 8208
  1458.8 64.5 %reduce-scatter.44.cloned.1.call-done = f32[2,16,256]{2,1,0:T(8,128)} async-done(((f32[2,16,2048]{2,1,0:T(8,128)}), f32[2,16,256]{2,1,0:T(8,128)}) %reduce-scatter.44.cloned.1.call-update) | async-done | bytes 32784 | tf_op jit(solution)/shard_map/reduce_scatter | solution.py:257
  1525.0 64.7 %reduce-scatter.42.cloned.1.call-done = f32[2,64,256]{2,1,0:T(8,128)} async-done(((f32[2,64,2048]{2,1,0:T(8,128)}), f32[2,64,256]{2,1,0:T(8,128)}) %reduce-scatter.42.cloned.1.call-update) | async-done | bytes 131088 | tf_op jit(solution)/shard_map/reduce_scatter | solution.py:255
  1591.7 66.2 %reduce-scatter.40.cloned.1.call-done = f32[2,256,96]{1,2,0:T(8,128)} async-done(((f32[2,2048,96]{1,2,0:T(8,128)}), f32[2,256,96]{1,2,0:T(8,128)}) %reduce-scatter.40.cloned.1.call-update) | async-done | bytes 196624 | tf_op jit(solution)/shard_map/reduce_scatter | solution.py:254
  1659.7 283.8 %reduce-scatter.38.cloned.1.call-done = f32[128,4096]{0,1:T(8,128)} async-done(((f32[1024,4096]{0,1:T(8,128)}), f32[128,4096]{0,1:T(8,128)}) %reduce-scatter.38.cloned.1.call-update) | async-done | bytes 2097168 | tf_op jit(solution)/shard_map/reduce_scatter | solution.py:251
  1955.3 9.3 reduce-scatter.66.cloned.1.call-done
  1966.0 20.7 reduce-scatter.60.cloned.1.call-done
  1988.0 20.6 reduce-scatter.54.cloned.1.call-done
  2010.0 20.5 reduce-scatter.50.cloned.1.call-done
  2032.1 20.5 reduce-scatter.62.cloned.1.call-done
  2054.1 20.4 reduce-scatter.56.cloned.1.call-done
  2076.0 32.7 %all-reduce.97.cloned.1.call-done = f32[2,256,96]{2,0,1:T(2,128)} async-done(((f32[2,256,96]{2,0,1:T(2,128)}), f32[2,256,96]{2,0,1:T(2,128)}) %all-reduce.97.cloned.1.call-update) | async-done | bytes 196624
  2110.2 33.1 %reduce-scatter.46.cloned.1.call-done = f32[32,4096]{1,0:T(8,128)} async-done(((f32[128,4096]{1,0:T(8,128)}), f32[32,4096]{1,0:T(8,128)}) %reduce-scatter.46.cloned.1.call-update) | async-done | bytes 524304
  (2435 shorter events, 1061.2 us)
Async XLA Ops:
  7.2 146.9 %copy-start = (bf16[1,128,1024]{2,1,0:T(8,128)(2,1)S(1)}, bf16[1,128,1024]{2,1,0:T(8,128)(2,1)}, u32[]{:S(2)}) copy-start(bf16[1,128,1024]{2,1,0:T(8,128)(2,1)} %param.35) | copy-start | bytes 786436
  7.2 146.9 %all-gather.8.cloned.1.call-start = ((), (), s32[]{:S(2)}) async-start(), calls=%async_computation.15 | async-start | bytes 9437184 | tf_op jit(solution)/shard_map/all_gather | solution.py:150
  7.9 180.8 %all-gather.10.cloned.1.call-start = ((), (), s32[]{:S(2)}) async-start(), calls=%async_computation.16 | async-start | bytes 1769472 | tf_op jit(solution)/shard_map/all_gather | solution.py:154
  8.7 219.9 %all-gather.12.cloned.1.call-start = ((), (), s32[]{:S(2)}) async-start(), calls=%async_computation.17 | async-start | bytes 1179648 | tf_op jit(solution)/shard_map/all_gather | solution.py:155
  9.4 1260.0 %reduce-scatter.64.cloned.1.call-start = ((), (), s32[]{:S(2)}) async-start(), calls=%async_computation.31 | async-start | bytes 1179648
  42.4 122.7 %copy-start.40 = (f32[1,1,2048]{2,1,0:T(1,128)}, f32[1,1,2048]{2,1,0:T(1,128)S(1)}, u32[]{:S(2)}) copy-start(f32[1,1,2048]{2,1,0:T(1,128)S(1)} %get-tuple-element.1946) | copy-start | bytes 24580
  42.4 122.7 %copy-start.42 = (f32[1,1,2048]{2,1,0:T(1,128)}, f32[1,1,2048]{2,1,0:T(1,128)S(1)}, u32[]{:S(2)}) copy-start(f32[1,1,2048]{2,1,0:T(1,128)S(1)} %get-tuple-element.1947) | copy-start | bytes 24580
  42.4 122.7 %copy-start.44 = (f32[1,1,2048]{2,1,0:T(1,128)}, f32[1,1,2048]{2,1,0:T(1,128)S(1)}, u32[]{:S(2)}) copy-start(f32[1,1,2048]{2,1,0:T(1,128)S(1)} %get-tuple-element.1948) | copy-start | bytes 24580
  42.4 122.7 %copy-start.46 = (f32[1,1,2048]{2,1,0:T(1,128)}, f32[1,1,2048]{2,1,0:T(1,128)S(1)}, u32[]{:S(2)}) copy-start(f32[1,1,2048]{2,1,0:T(1,128)S(1)} %get-tuple-element.1949) | copy-start | bytes 24580
  42.4 122.7 %copy-start.48 = (f32[1,1,2048]{2,1,0:T(1,128)}, f32[1,1,2048]{2,1,0:T(1,128)S(1)}, u32[]{:S(2)}) copy-start(f32[1,1,2048]{2,1,0:T(1,128)S(1)} %get-tuple-element.1950) | copy-start | bytes 24580
  42.4 122.7 %copy-start.50 = (f32[1,1,2048]{2,1,0:T(1,128)}, f32[1,1,2048]{2,1,0:T(1,128)S(1)}, u32[]{:S(2)}) copy-start(f32[1,1,2048]{2,1,0:T(1,128)S(1)} %get-tuple-element.1951) | copy-start | bytes 24580
  42.4 122.7 %copy-start.52 = (f32[1,1,2048]{2,1,0:T(1,128)}, f32[1,1,2048]{2,1,0:T(1,128)S(1)}, u32[]{:S(2)}) copy-start(f32[1,1,2048]{2,1,0:T(1,128)S(1)} %get-tuple-element.1952) | copy-start | bytes 24580
  127.9 267.1 %copy-start.19 = (f32[2,16,2048]{2,1,0:T(8,128)}, f32[2,16,2048]{2,1,0:T(8,128)S(1)}, u32[]{:S(2)}) copy-start(f32[2,16,2048]{2,1,0:T(8,128)S(1)} %all_gather.66) | copy-start | bytes 786436
  158.8 3.1 collective-permute-start
  160.1 4.8 collective-permute-start.1
  1198.2 128.4 %reduce-scatter.58.cloned.1.call-start = ((), (), s32[]{:S(2)}) async-start(), calls=%async_computation.28 | async-start | bytes 1179648
  1224.1 168.2 %reduce-scatter.52.cloned.1.call-start = ((), (), s32[]{:S(2)}) async-start(), calls=%async_computation.25 | async-start | bytes 1179648
  1239.1 219.6 %reduce-scatter.48.cloned.1.call-start = ((), (), s32[]{:S(2)}) async-start(), calls=%async_computation.23 | async-start | bytes 1179648
  1245.0 278.3 %reduce-scatter.44.cloned.1.call-start = ((), (), s32[]{:S(2)}) async-start(), calls=%async_computation.21 | async-start | bytes 294912 | tf_op jit(solution)/shard_map/reduce_scatter | solution.py:257
  1245.7 344.0 %reduce-scatter.42.cloned.1.call-start = ((), (), s32[]{:S(2)}) async-start(), calls=%async_computation.20 | async-start | bytes 1179648 | tf_op jit(solution)/shard_map/reduce_scatter | solution.py:255
  1248.4 409.5 %reduce-scatter.40.cloned.1.call-start = ((), (), s32[]{:S(2)}) async-start(), calls=%async_computation.19 | async-start | bytes 1769472 | tf_op jit(solution)/shard_map/reduce_scatter | solution.py:254
  1252.4 691.1 %reduce-scatter.38.cloned.1.call-start = ((), (), s32[]{:S(2)}) async-start(), calls=%async_computation.18 | async-start | bytes 18874368 | tf_op jit(solution)/shard_map/reduce_scatter | solution.py:251
  1254.3 6.0 collective-permute-start.3
  1257.3 3.8 collective-permute-start.2
  1269.3 695.3 %reduce-scatter.66.cloned.1.call-start = ((), (), s32[]{:S(2)}) async-start(), calls=%async_computation.32 | async-start | bytes 163840
  1269.9 716.7 %reduce-scatter.60.cloned.1.call-start = ((), (), s32[]{:S(2)}) async-start(), calls=%async_computation.29 | async-start | bytes 163840
  1326.6 682.0 %reduce-scatter.54.cloned.1.call-start = ((), (), s32[]{:S(2)}) async-start(), calls=%async_computation.26 | async-start | bytes 163840
  1392.4 638.1 %reduce-scatter.50.cloned.1.call-start = ((), (), s32[]{:S(2)}) async-start(), calls=%async_computation.24 | async-start | bytes 163840
  1458.7 593.8 %reduce-scatter.62.cloned.1.call-start = ((), (), s32[]{:S(2)}) async-start(), calls=%async_computation.30 | async-start | bytes 163840
  1525.0 549.4 %reduce-scatter.56.cloned.1.call-start = ((), (), s32[]{:S(2)}) async-start(), calls=%async_computation.27 | async-start | bytes 163840
  1591.6 517.1 %all-reduce.97.cloned.1.call-start = ((), (), s32[]{:S(2)}) async-start(), calls=%async_computation.33 | async-start | bytes 524288
  1659.7 483.6 %reduce-scatter.46.cloned.1.call-start = ((), (), s32[]{:S(2)}) async-start(), calls=%async_computation.22 | async-start | bytes 2621440
  (80 other events, 577.5 us)
Sparse Core Ops, SparseCore 0:
  10.2 132.8 all-gather.7
  145.1 43.6 all-gather.9
  190.8 37.7 all-gather.11
  1198.3 62.1 reduce-scatter.63
  1264.2 62.3 reduce-scatter.57
  1329.8 62.4 reduce-scatter.51
  1396.2 62.4 reduce-scatter.47
  1462.6 60.6 reduce-scatter.43
  1526.6 63.0 reduce-scatter.41
  1593.4 64.3 reduce-scatter.39
  1661.6 281.7 reduce-scatter.37
  1945.9 18.6 reduce-scatter.65
  1967.0 19.5 reduce-scatter.59
  1989.0 19.5 reduce-scatter.53
  2010.9 19.5 reduce-scatter.49
  2032.9 19.5 reduce-scatter.61
  2054.8 19.5 reduce-scatter.55
  2076.7 31.9 all-reduce.96
  2111.8 31.4 reduce-scatter.45
where the time goes:
time: 2170 us; the launch traced here: 2150 us
  waiting for transfers between devices  910 us (42%)
  local copies, waits for them, and re-layouts  432 us (20%)
  other arithmetic  294 us (14%)
  matrix products  291 us (13%)
  blocking collectives  188 us (9%)
    unnamed x31, waiting for transfers between devices  369 us
    reduce_scatter x1, waiting for transfers between devices, shards(): lax.psum_scatter(weight_back, 'dp', scatter_dimension=0, tiled=True)  284 us
    squeeze x256, local copies, waits for them, and re-layouts, forward_summary(): (state, elapsed), _ = lax.scan(forward_advance, start, blocks)  154 us
    dot_general x512, matrix products, block_advance(): results.append(jnp.dot(read_part[place], state, precision=HIGH))  149 us
    dynamic_update_slice x160, other arithmetic, block_scan(): lax.scan(jax.checkpoint(block_advance), state_in, blocks)  106 us
    reduce_scatter x1, waiting for transfers between devices, shards(): lax.psum_scatter(param_backs[2], 'dp', scatter_dimension=1, tiled=True)  66.2 us
    reduce_scatter x1, waiting for transfers between devices, shards(): lax.psum_scatter(param_backs[3], 'dp', scatter_dimension=2, tiled=True)  64.7 us
    reduce_scatter x1, waiting for transfers between devices, shards(): lax.psum_scatter(rates_back, 'dp', scatter_dimension=2, tiled=True)  64.5 us
  transfers between devices with their start and end apart: 23, of which 19 were waited for; matrix products, arithmetic and copies ran while one was open for 5% of the time, Pallas kernels for 0%

commit v1 on v0

--- a/solution.py
+++ b/solution.py
@@ -12,22 +12,6 @@
 
 
 HIGH = lax.Precision.HIGHEST
-
-
-def prefix(part, axis, combine, identity, reverse):
-    count = lax.axis_size(axis)
-    place = lax.axis_index(axis)
-    ahead = count - 1 - place if reverse else place
-    gathered = jax.tree.map(lambda a: lax.all_gather(a, axis), part)
-    state = jax.tree.map(lambda a, e: jnp.zeros_like(a) + jnp.asarray(e, a.dtype), part, identity)
-
-    def one(step, state):
-        source = count - 1 - step if reverse else step
-        return combine(
-            state, jax.tree.map(lambda a: lax.dynamic_index_in_dim(a, source, 0, False), gathered)
-        )
-
-    return lax.fori_loop(0, ahead, one, state)
 
 
 def extended(x, sides, width):
@@ -41,10 +25,6 @@
         after = lax.ppermute(first, axis, down)
         x = jnp.concatenate([before, x, after], axis=dim)
     return x
-
-
-def combine_pair(earlier, later):
-    return (earlier[0] * later[0], later[0] * earlier[1] + later[1])
 
 
 def block_scan(state_in, active, steps, inputs, reads, log_rate, skip_gain):
@@ -127,12 +107,44 @@
     return jnp.sum(parts, axis=0)
 
 
-def pass_states(rising, falling):
-    rise_start = (jnp.ones_like(rising[0]), jnp.zeros_like(rising[1]))
-    below = prefix(rising, "seq", combine_pair, rise_start, False)
-    fall_start = (jnp.ones_like(falling[0]), jnp.zeros_like(falling[1]))
-    above = prefix(falling, "seq", combine_pair, fall_start, True)
-    return (below[1], above[1])
+def chain(decays, states, reverse):
+    count = lax.axis_size("seq")
+    place = lax.axis_index("seq")
+    ahead = count - 1 - place if reverse else place
+    state = jnp.zeros_like(states[0])
+    for step in range(count - 1):
+        source = count - 1 - step if reverse else step
+        state = jnp.where(step < ahead, decays[source] * state + states[source], state)
+    return state
+
+
+def pack_rows(arrays, multiple):
+    fw, fb, sw, tw, tb, lr, sg = arrays
+    channels = fb.shape[1]
+    rows = [fw, fb, sw.transpose(0, 2, 1), tw, tb, lr, sg]
+    rows = [row.reshape(-1, channels) for row in rows]
+    used = sum(row.shape[0] for row in rows)
+    pad = -used % multiple
+    return jnp.concatenate(rows + [jnp.zeros((pad, channels), jnp.float32)], axis=0)
+
+
+def unpack_rows(packed):
+    channels = packed.shape[1]
+    sizes = (2 * K, 2, 2 * (R + 2 * N), 2 * R, 2, 2 * N, 2)
+    parts = []
+    start = 0
+    for size in sizes:
+        parts.append(packed[start : start + size])
+        start += size
+    return (
+        parts[0].reshape(2, K, channels),
+        parts[1],
+        parts[2].reshape(2, R + 2 * N, channels).transpose(0, 2, 1),
+        parts[3].reshape(2, R, channels),
+        parts[4],
+        parts[5].reshape(2, N, channels),
+        parts[6],
+    )
 
 
 def shards(
@@ -148,15 +160,12 @@
     skip_gain,
 ):
     full_weight = lax.all_gather(input_weight, "dp", axis=0, tiled=True)
-    params = (
-        lax.all_gather(filter_weight, "dp", axis=2, tiled=True),
-        lax.all_gather(filter_bias, "dp", axis=1, tiled=True),
-        lax.all_gather(scan_weight, "dp", axis=1, tiled=True),
-        lax.all_gather(step_weight, "dp", axis=2, tiled=True),
-        lax.all_gather(step_bias, "dp", axis=1, tiled=True),
-        lax.all_gather(log_rate, "dp", axis=2, tiled=True),
-        lax.all_gather(skip_gain, "dp", axis=1, tiled=True),
-    )
+    packed = pack_rows(
+        (filter_weight, filter_bias, scan_weight, step_weight, step_bias, log_rate, skip_gain), 8
+    )
+    spread = lax.all_gather(packed, "dp", axis=0)
+    params = unpack_rows(spread.transpose(1, 0, 2).reshape(packed.shape[0], -1))
+    all_tokens = lax.all_gather(tokens[0], "seq", axis=0, tiled=True)
     inputs = tokens[0]
     projected = jnp.dot(inputs, full_weight, preferred_element_type=jnp.float32).astype(
         jnp.bfloat16
@@ -184,7 +193,9 @@
         prepared_list.append(prepared)
         prep_pulls.append(prep_pull)
         summaries.append(forward_summary(prepared[0], prepared[1], prepared[2], params[5][which]))
-    start_rise, start_fall = pass_states(summaries[0], summaries[1])
+    told = lax.all_gather(jnp.stack([part for pair in summaries for part in pair]), "seq", axis=0)
+    start_rise = chain(told[:, 0], told[:, 1], False)
+    start_fall = chain(told[:, 2], told[:, 3], True)
     starts = (start_rise, start_fall)
     outputs = []
     scan_pulls = []
@@ -216,7 +227,9 @@
                 prepared_list[which][1], prepared_list[which][3], directed[which], params[5][which]
             )
         )
-    late_one, late_zero = pass_states((summaries[1][0], flows[1]), (summaries[0][0], flows[0]))
+    late_told = lax.all_gather(jnp.stack(flows), "seq", axis=0)
+    late_one = chain(told[:, 2], late_told[:, 1], False)
+    late_zero = chain(told[:, 0], late_told[:, 0], True)
     lates = (late_zero, late_one)
     back_padded = jnp.zeros_like(padded)
     param_backs = [jnp.zeros_like(param) for param in params[:5]]
@@ -232,8 +245,8 @@
         param_backs = [older + newer for older, newer in zip(param_backs, more[1:])]
         rate_rows.append(backs[5])
         skip_rows.append(backs[6])
-    packed = jnp.concatenate([back_padded[:rim], back_padded[-rim:]], axis=0)
-    returned = extended(packed, (("seq", 0),), rim)
+    rims = jnp.concatenate([back_padded[:rim], back_padded[-rim:]], axis=0)
+    returned = extended(rims, (("seq", 0),), rim)
     middle = back_padded[rim:-rim]
     back_values = jnp.concatenate(
         [middle[:rim] + returned[:rim], middle[rim:-rim], middle[-rim:] + returned[-rim:]], axis=0
@@ -242,31 +255,32 @@
     tokens_back = lax.dot_general(
         back_projected, full_weight, (((1,), (1,)), ((), ())), preferred_element_type=jnp.float32
     ).astype(jnp.bfloat16)
+    groups, peers = lax.axis_size("dp"), lax.axis_size("seq")
+    all_back = lax.all_gather(back_projected, "seq", axis=0, tiled=True)
+    depth = all_tokens.shape[1]
+    shared = all_tokens.reshape(all_tokens.shape[0], groups, peers, depth // (groups * peers))
+    mine = lax.dynamic_index_in_dim(shared, lax.axis_index("seq"), 2, False)
     weight_back = lax.dot_general(
-        inputs, back_projected, (((0,), (0,)), ((), ())), preferred_element_type=jnp.float32
-    )
+        mine.reshape(mine.shape[0], -1),
+        all_back,
+        (((0,), (0,)), ((), ())),
+        preferred_element_type=jnp.float32,
+    ).astype(jnp.bfloat16)
+    wide = weight_back.shape[1]
+    weight_back = weight_back.reshape(groups, -1, wide)
     rates_back = jnp.stack(rate_rows)
     skip_back = jnp.stack(skip_rows)
-    group_sums = (
-        lax.psum_scatter(weight_back, "dp", scatter_dimension=0, tiled=True),
-        lax.psum_scatter(param_backs[0], "dp", scatter_dimension=2, tiled=True),
-        lax.psum_scatter(param_backs[1], "dp", scatter_dimension=1, tiled=True),
-        lax.psum_scatter(param_backs[2], "dp", scatter_dimension=1, tiled=True),
-        lax.psum_scatter(param_backs[3], "dp", scatter_dimension=2, tiled=True),
-        lax.psum_scatter(param_backs[4], "dp", scatter_dimension=1, tiled=True),
-        lax.psum_scatter(rates_back, "dp", scatter_dimension=2, tiled=True),
-        lax.psum_scatter(skip_back, "dp", scatter_dimension=1, tiled=True),
-    )
-    sums = (
-        lax.psum_scatter(group_sums[0], "seq", scatter_dimension=0, tiled=True),
-        lax.psum_scatter(group_sums[1], "seq", scatter_dimension=2, tiled=True),
-        lax.psum_scatter(group_sums[2], "seq", scatter_dimension=1, tiled=True),
-        lax.psum_scatter(group_sums[3], "seq", scatter_dimension=1, tiled=True),
-        lax.psum_scatter(group_sums[4], "seq", scatter_dimension=2, tiled=True),
-        lax.psum_scatter(group_sums[5], "seq", scatter_dimension=1, tiled=True),
-        lax.psum_scatter(group_sums[6], "seq", scatter_dimension=2, tiled=True),
-        lax.psum_scatter(group_sums[7], "seq", scatter_dimension=1, tiled=True),
-    )
+    own = skip_back.shape[1] // (groups * peers)
+    small = pack_rows((*param_backs, rates_back, skip_back), wide // own).astype(jnp.bfloat16)
+    height = small.shape[0]
+    small = small.reshape(height, groups, peers, own).transpose(2, 1, 0, 3)
+    small = lax.all_to_all(small.reshape(peers, groups, -1, wide), "seq", 0, 0)
+    small = jnp.sum(small.astype(jnp.float32), axis=0).astype(jnp.bfloat16)
+    joined = jnp.concatenate([weight_back, small], axis=1)
+    joined = lax.all_to_all(joined, "dp", 0, 0)
+    joined = jnp.sum(joined.astype(jnp.float32), axis=0)
+    edge = weight_back.shape[1]
+    sums = (joined[:edge], *unpack_rows(joined[edge:].reshape(height, own)))
     return (
         mixed[None],
         tokens_back[None],

time: 2170 us -> 1350 us (0.62)
  waiting for transfers between devices: 910 us -> 292 us
  blocking collectives: 188 us -> 0 us
  local copies, waits for them, and re-layouts: 432 us -> 408 us
    reduce_scatter x4 -> x0, waiting for transfers between devices: 479 us -> none  [the longest x1 284 us: shards(): lax.psum_scatter(weight_back, 'dp', scatter_dimension=0, tiled=True)]
    unnamed x31 -> x6, waiting for transfers between devices: 369 us -> 0.78 us
    all_gather x11 -> x0, blocking collectives: 188 us -> none  [the longest x6 43.2 us: prefix(): gathered = jax.tree.map(lambda a: lax.all_gather(a, axis), part)]
    all_gather x1, waiting for transfers between devices: 0.01 us -> 120 us  [shards(): full_weight = lax.all_gather(input_weight, 'dp', axis=0, tiled=True)]
    all_to_all x0 -> x2, waiting for transfers between devices: none -> 71.2 us  [the longest x1 52 us: shards(): joined = lax.all_to_all(joined, 'dp', 0, 0)]
    all_gather x2 -> x5, waiting for transfers between devices: 58 us -> 98.9 us  [the longest x1 61.1 us: shards(): spread = lax.all_gather(packed, 'dp', axis=0)]
    squeeze x256, local copies, waits for them, and re-layouts: 154 us -> 121 us  [forward_summary(): (state, elapsed), _ = lax.scan(forward_advance, start, blocks)]
    concatenate x0 -> x12, local copies, waits for them, and re-layouts: none -> 26.8 us  [pack_rows(): jnp.concatenate(rows + [jnp.zeros((pad, channels), jnp.float32)], axis=0)]
  transfers between devices with their start and end apart: 23 -> 12, of which waited for: 19 -> 7; matrix products, arithmetic and copies ran while one was open for 5% -> 34% of each run, Pallas kernels for 0% -> 0%
where the time goes in v1:
time: 1350 us; the launch traced here: 1330 us
  local copies, waits for them, and re-layouts  408 us (30%)
  other arithmetic  303 us (22%)
  waiting for transfers between devices  292 us (22%)
  matrix products  280 us (21%)
  starting transfers between devices  19.1 us (1%)
  between operations  16.1 us (1%)
    dot_general x512, matrix products, block_advance(): results.append(jnp.dot(read_part[place], state, precision=HIGH))  149 us
    squeeze x256, local copies, waits for them, and re-layouts, forward_summary(): (state, elapsed), _ = lax.scan(forward_advance, start, blocks)  121 us
    all_gather x1, waiting for transfers between devices, shards(): full_weight = lax.all_gather(input_weight, 'dp', axis=0, tiled=True)  120 us
    dynamic_update_slice x160, other arithmetic, block_scan(): lax.scan(jax.checkpoint(block_advance), state_in, blocks)  95.9 us
    all_gather x1, waiting for transfers between devices, shards(): spread = lax.all_gather(packed, 'dp', axis=0)  61.1 us
    all_to_all x1, waiting for transfers between devices, shards(): joined = lax.all_to_all(joined, 'dp', 0, 0)  52 us
    dot_general x32, matrix products, adjoint_advance(): jnp.einsum('qn,qne->ne', read_part, weights, precision=HIGH)  47.7 us
    dot_general x32, matrix products, forward_advance(): local = jnp.einsum('qn,qne->ne', input_part, weights, precision=HIGH)  47.7 us
  transfers between devices with their start and end apart: 12, of which 7 were waited for; matrix products, arithmetic and copies ran while one was open for 34% of the time, Pallas kernels for 0%

profile of v1, /device:TPU:0, one launch (start us, length us, event | category | flops | bytes accessed | tf_op | source)
XLA Modules:
  0.0 1329.3 jit_solution(9585312716252868399)
XLA Ops:
  7.9 9.1 concatenate.40
  17.9 61.1 %all-gather.15.cloned.1.call-done = f32[2944,256]{1,0:T(8,128)} async-done(((f32[368,256]{1,0:T(8,128)}), f32[2944,256]{1,0:T(8,128)}) %all-gather.15.cloned.1.call-update) | async-done | bytes 3014672 | tf_op jit(solution)/shard_map/all_gather | solution.py:166
  84.7 120.0 %all-gather.11.cloned.1.call-done = bf16[1024,4096]{1,0:T(8,128)(2,1)} async-done(((bf16[128,4096]{1,0:T(8,128)(2,1)}), bf16[1024,4096]{1,0:T(8,128)(2,1)}) %all-gather.11.cloned.1.call-update) | async-done | bytes 8388624 | tf_op jit(solution)/shard_map/all_gather | solution.py:162
  204.7 4.8 convolution_convert_fusion.1
  229.0 59.6 %while.136 = (s32[]{:T(128)}, f32[16,2048]{1,0:T(8,128)S(1)}, f32[2048]{0:T(1024)S(1)}, f32[16,8,2048]{2,1,0:T(8,128)}, f32[16,2048]{1,0:T(8,128)S(1)}, /*index=...) while((s32[]{:T(128)}, f32[16,2048]{1,0:T(8,128)S(1)}, ...), condition=%wide.region_2.4_spmd.clone, body=%wide.region_0.3_spmd.clone.sunk | while | flops 3952643 | bytes 3664512 | solution.py:89
  294.0 5.3 rev.30
  299.5 8.9 rev.32
  308.4 59.4 %while.137 = (s32[]{:T(128)}, f32[16,2048]{1,0:T(8,128)S(1)}, f32[2048]{0:T(1024)S(1)}, f32[16,8,2048]{2,1,0:T(8,128)}, f32[16,2048]{1,0:T(8,128)S(1)}, /*index=...) while((s32[]{:T(128)}, f32[16,2048]{1,0:T(8,128)S(1)}, ...), condition=%wide.region_5.7_spmd.clone, body=%wide.region_3.6_spmd.clone.sunk | while | flops 3952643 | bytes 3664512 | solution.py:89
  369.2 22.9 %all-gather.17.cloned.1.call-done = f32[16,16,2048]{2,1,0:T(8,128)} async-done(((f32[4,16,2048]{2,1,0:T(8,128)}), f32[16,16,2048]{2,1,0:T(8,128)}) %all-gather.17.cloned.1.call-update) | async-done | bytes 2097168 | tf_op jit(solution)/shard_map/all_gather | solution.py:196
  395.3 101.3 %while.132 = (s32[]{:T(128)}, f32[16,2048]{1,0:T(8,128)S(1)}, f32[16,8,2048]{2,1,0:T(8,128)S(1)}, f32[16,16,2048]{2,1,0:T(8,128)}, f32[16,8,2048]{2,1,0:T(8,128)...) while((s32[]{:T(128)}, f32[16,2048]{1,0:T(8,128)S(1)}, ...), condition=%wide.region_7.9_spmd, body=%wide.region_6.8_spmd.sunk | while | flops 5816329 | bytes 3823917 | solution.py:51
  499.3 110.9 %while.133 = (s32[]{:T(128)}, f32[16,2048]{1,0:T(8,128)S(1)}, f32[16,8,2048]{2,1,0:T(8,128)S(1)}, f32[16,16,2048]{2,1,0:T(8,128)}, f32[16,8,2048]{2,1,0:T(8,128)...) while((s32[]{:T(128)}, f32[16,2048]{1,0:T(8,128)S(1)}, ...), condition=%wide.region_9.11_spmd, body=%wide.region_8.10_spmd.sunk | while | flops 5816329 | bytes 3823917 | solution.py:51
  610.3 5.2 rev.34
  615.5 3.9 fusion.170
  621.0 66.0 %while.134 = (s32[]{:T(128)}, f32[2048]{0:T(1024)S(1)}, f32[16,16,2048]{2,1,0:T(8,128)}, f32[16,8,2048]{2,1,0:T(8,128)}, f32[16,8,16]{2,1,0:T(8,128)}, /*index=5...) while((s32[]{:T(128)}, f32[2048]{0:T(1024)S(1)}, f32[16,16,2048]{2,1,0:T(8,128)}, ...), condition=%wide.region_12.14_spmd, body=%wide.region_10.13_spmd.sunk | while | flops 3801090 | bytes 3304553 | solution.py:106
  687.0 8.9 rev.35
  697.5 55.1 %while.135 = (s32[]{:T(128)}, f32[2048]{0:T(1024)S(1)}, f32[16,16,2048]{2,1,0:T(8,128)}, f32[16,8,2048]{2,1,0:T(8,128)}, f32[16,8,16]{2,1,0:T(8,128)S(1)}, /*ind...) while((s32[]{:T(128)}, f32[2048]{0:T(1024)S(1)}, f32[16,16,2048]{2,1,0:T(8,128)}, ...), condition=%wide.region_16.18_spmd, body=%wide.region_14.17_spmd.sunk | while | flops 3801090 | bytes 3304553 | solution.py:106
  759.5 14.9 %all-gather.19.cloned.1.call-done = f32[8,16,2048]{2,1,0:T(8,128)} async-done(((f32[2,16,2048]{2,1,0:T(8,128)}), f32[8,16,2048]{2,1,0:T(8,128)}) %all-gather.19.cloned.1.call-update) | async-done | bytes 1048592 | tf_op jit(solution)/shard_map/all_gather | solution.py:230
  778.2 160.0 %while.138 = (s32[]{:T(128)}, f32[16,2048]{1,0:T(8,128)S(1)}, f32[2048]{0:T(1024)S(1)}, f32[16,2048]{1,0:T(8,128)S(1)}, f32[16,8,2048]{2,1,0:T(8,128)}, /*index=...) while((s32[]{:T(128)}, f32[16,2048]{1,0:T(8,128)S(1)}, ...), condition=%wide.region_44.46_spmd.clone, body=%wide.region_18.45_spmd.clone.sunk | while | flops 12701316 | bytes 8625508 | solution.py:51
  941.7 202.2 %while.139 = (s32[]{:T(128)}, f32[16,2048]{1,0:T(8,128)}, f32[2048]{0:T(1024)S(1)}, f32[16,2048]{1,0:T(8,128)S(1)}, f32[16,8,2048]{2,1,0:T(8,128)}, /*index=5*/f...) while((s32[]{:T(128)}, f32[16,2048]{1,0:T(8,128)}, ...), condition=%wide.region_71.73_spmd.clone, body=%wide.region_45.72_spmd.clone.sunk | while | flops 12701316 | bytes 8618340 | solution.py:51
  1144.0 9.0 rev.39
  1153.0 3.6 fusion.173
  1162.2 7.1 rev.36
  1172.5 3.6 multiply_reduce_fusion.57
  1178.6 3.2 collective-permute-start.2
  1203.0 6.5 concatenate.52
  1212.5 4.8 reshape.967
  1219.4 5.2 all-to-all-start
  1225.6 19.1 %all-to-all-done = bf16[4,8,6,4096]{3,1,2,0:T(8,128)(2,1)S(1)} async-done(((bf16[4,8,6,4096]{3,1,2,0:T(8,128)(2,1)}), bf16[4,8,6,4096]{3,1,2,0:T(8,128)(2,1)S(1)}, u32[]{:S(2)}, u32[]{:S(2)}) %all-to-all-start) | async-done | bytes 1572896 | tf_op jit(solution)/shard_map/all_to_all | solution.py:277
  1245.3 3.4 convolution_convert_fusion
  1250.6 6.0 all-to-all-start.1
  1256.6 7.0 fusion.102
  1263.6 52.0 %all-to-all-done.1 = bf16[8,38,4096]{2,1,0:T(8,128)(2,1)} async-done(((bf16[8,38,4096]{2,1,0:T(8,128)(2,1)}), bf16[8,38,4096]{2,1,0:T(8,128)(2,1)}, u32[]{:S(2)}, u32[]{:S(2)}) %all-to-all-start.1) | async-done | bytes 2490400 | tf_op jit(solution)/shard_map/all_to_all | solution.py:280
  (2391 shorter events, 905.9 us)
Async XLA Ops:
  7.2 71.8 %all-gather.15.cloned.1.call-start = ((), (), s32[]{:S(2)}) async-start(), calls=%async_computation.4 | async-start | bytes 3391488 | tf_op jit(solution)/shard_map/all_gather | solution.py:166
  17.1 187.7 %copy-start.19 = (bf16[1,128,1024]{2,1,0:T(8,128)(2,1)S(1)}, bf16[1,128,1024]{2,1,0:T(8,128)(2,1)}, u32[]{:S(2)}) copy-start(bf16[1,128,1024]{2,1,0:T(8,128)(2,1)} %param.27) | copy-start | bytes 786436
  17.1 187.6 %all-gather.11.cloned.1.call-start = ((), (), s32[]{:S(2)}) async-start(), calls=%async_computation.2 | async-start | bytes 9437184 | tf_op jit(solution)/shard_map/all_gather | solution.py:162
  17.8 374.3 %all-gather.17.cloned.1.call-start = ((), (), s32[]{:S(2)}) async-start(), calls=%async_computation.5 | async-start | bytes 2621440 | tf_op jit(solution)/shard_map/all_gather | solution.py:196
  84.7 136.5 %copy-start.48 = (f32[1,1,2048]{2,1,0:T(1,128)}, f32[1,1,2048]{2,1,0:T(1,128)S(1)}, u32[]{:S(2)}) copy-start(f32[1,1,2048]{2,1,0:T(1,128)S(1)} %get-tuple-element.1629) | copy-start | bytes 24580
  84.7 136.5 %copy-start.50 = (f32[1,1,2048]{2,1,0:T(1,128)}, f32[1,1,2048]{2,1,0:T(1,128)S(1)}, u32[]{:S(2)}) copy-start(f32[1,1,2048]{2,1,0:T(1,128)S(1)} %get-tuple-element.1630) | copy-start | bytes 24580
  84.7 136.5 %copy-start.52 = (f32[1,1,2048]{2,1,0:T(1,128)}, f32[1,1,2048]{2,1,0:T(1,128)S(1)}, u32[]{:S(2)}) copy-start(f32[1,1,2048]{2,1,0:T(1,128)S(1)} %get-tuple-element.1631) | copy-start | bytes 24580
  84.7 136.5 %copy-start.54 = (f32[1,1,2048]{2,1,0:T(1,128)}, f32[1,1,2048]{2,1,0:T(1,128)S(1)}, u32[]{:S(2)}) copy-start(f32[1,1,2048]{2,1,0:T(1,128)S(1)} %get-tuple-element.1632) | copy-start | bytes 24580
  204.7 8.7 copy-start.16
  209.5 10.7 copy-start.12
  210.3 10.0 collective-permute-start
  212.2 8.1 collective-permute-start.1
  217.7 7.6 copy-start.8
  291.5 7.9 copy-start.44
  308.4 59.5 %copy-start.31 = (f32[1,16,2048]{2,1,0:T(8,128)S(1)}, f32[1,16,2048]{2,1,0:T(8,128)}, u32[]{:S(2)}) copy-start(f32[1,16,2048]{2,1,0:T(8,128)} %neg.60) | copy-start | bytes 393220
  367.9 27.4 %copy-start.38 = (f32[16,8,16]{2,1,0:T(8,128)}, f32[16,8,16]{2,1,0:T(8,128)S(1)}, u32[]{:S(2)}) copy-start(f32[16,8,16]{2,1,0:T(8,128)S(1)} %get-tuple-element.2978) | copy-start | bytes 24580
  368.8 405.6 %all-gather.19.cloned.1.call-start = ((), (), s32[]{:S(2)}) async-start(), calls=%async_computation.6 | async-start | bytes 1310720 | tf_op jit(solution)/shard_map/all_gather | solution.py:230
  610.2 5.2 copy-start.13
  757.6 467.0 %all-gather.21.cloned.1.call-start = ((), (), s32[]{:S(2)}) async-start(), calls=%async_computation.7 | async-start | bytes 1310720 | tf_op jit(solution)/shard_map/all_gather | solution.py:168
  759.4 485.8 %all-gather.13.cloned.1.call-start = ((), (), s32[]{:S(2)}) async-start(), calls=%async_computation.3 | async-start | bytes 5242880 | tf_op jit(solution)/shard_map/all_gather | solution.py:259
  1144.0 9.0 copy-start.2
  1153.0 5.9 copy-start.37
  1153.0 5.9 copy-start.35
  1160.2 12.1 copy-start.46
  1161.2 11.1 copy-start.76
  1162.2 10.2 copy-start.78
  1176.1 5.6 collective-permute-start.3
  1178.6 4.0 collective-permute-start.2
  1196.1 7.0 copy-start.14
  1219.4 25.3 %all-to-all-start = ((bf16[4,8,6,4096]{3,1,2,0:T(8,128)(2,1)}), bf16[4,8,6,4096]{3,1,2,0:T(8,128)(2,1)S(1)}, u32[]{:S(2)}, u32[]{:S(2)}) async-start(bf16[4,8,6,4096]{3,1,2,0:T(8,128)(2,1)} %copy.132), calls=%async_computation | async-start | bytes 3145728 | tf_op jit(solution)/shard_map/all_to_all | solution.py:277
  1250.6 6.0 copy-start
  1250.6 65.0 %all-to-all-start.1 = ((bf16[8,38,4096]{2,1,0:T(8,128)(2,1)}), bf16[8,38,4096]{2,1,0:T(8,128)(2,1)}, u32[]{:S(2)}, u32[]{:S(2)}) async-start(bf16[8,38,4096]{2,1,0:T(8,128)(2,1)} %pad_maximum_fusion), calls=%async_computation.1 | async-start | bytes 5242880 | tf_op jit(solution)/shard_map/all_to_all | solution.py:280
  (60 other events, 156.8 us)
Sparse Core Ops, SparseCore 0:
  17.2 61.7 all-gather.14
  81.1 123.5 all-gather.10
  368.9 23.1 all-gather.16
  757.7 16.7 all-gather.18
  775.8 16.8 all-gather.20
  1184.0 37.7 all-gather.12

commit v2 on v1

v2 whole, which is shorter than its diff:
```python
from functools import partial

import jax
import jax.numpy as jnp
from jax import lax
from jax.experimental import pallas as pl
from jax.experimental.pallas import tpu as pltpu
from jax.sharding import PartitionSpec as P

N = 16
K = 4
R = 64


HIGH = lax.Precision.HIGHEST


def extended(x, sides, width):
    for axis, dim in sides:
        peers, length = (lax.axis_size(axis), x.shape[dim])
        up = [(i, (i + 1) % peers) for i in range(peers - 1)]
        down = [(j, i) for i, j in up]
        last = lax.slice_in_dim(x, length - width, length, axis=dim)
        first = lax.slice_in_dim(x, 0, width, axis=dim)
        before = lax.ppermute(last, axis, up)
        after = lax.ppermute(first, axis, down)
        x = jnp.concatenate([before, x, after], axis=dim)
    return x


def prepare(padded, filter_weight, filter_bias, scan_weight, step_weight, step_bias, which):
    length = padded.shape[0] - 2 * (K - 1)
    filtered = filter_bias[which]
    for tap in range(K):
        start = tap if which == 0 else 2 * (K - 1) - tap
        filtered = filtered + filter_weight[which, tap] * padded[start : start + length]
    active = jax.nn.silu(filtered)
    coefficients = jnp.dot(active, scan_weight[which], precision=HIGH)
    steps = jax.nn.softplus(
        jnp.dot(coefficients[:, :R], step_weight[which], precision=HIGH) + step_bias[which]
    )
    return (active, steps, coefficients[:, R : R + N], coefficients[:, R + N :])


LANES = 128
TILE = 512
UNROLL = 4
LIMIT = 48 * 1024 * 1024


def row_of(ref, at):
    return ref[0, pl.ds(at, 1), :]


def summary_kernel(active, steps, back, inputs, reads, rate, state_out, flow_out, span_out):
    length = active.shape[1]
    falling = pl.program_id(0)
    repeat = rate.shape[2] // LANES
    rates = rate[0]

    def wide(ref, at):
        return jnp.concatenate([ref[0, at]] * repeat, axis=1)

    def place_of(t):
        return t + falling * (length - 1 - 2 * t)

    def one(t, carry):
        state, flow, span = carry
        at = place_of(t)
        step = row_of(steps, at)
        state = jnp.exp(step * rates) * state + (step * row_of(active, at)) * wide(inputs, at)
        end = place_of(length - 1 - t)
        flow = flow + row_of(back, end) * wide(reads, end)
        flow = jnp.exp(row_of(steps, end) * rates) * flow
        return (state, flow, span + step)

    zero = jnp.zeros(rates.shape, jnp.float32)
    start = (zero, zero, jnp.zeros((1, rates.shape[1]), jnp.float32))
    state, flow, span = lax.fori_loop(0, length, one, start, unroll=UNROLL)
    state_out[0] = state
    flow_out[0] = flow
    span_out[0] = jnp.exp(span * rates)


def scan_kernel(
    active, steps, back, inputs, reads, rate, skip, first, late,
    result, active_back, steps_back, inputs_back, reads_back, rate_back, skip_back, held,
):
    length = active.shape[1]
    falling = pl.program_id(0)
    repeat = rate.shape[2] // LANES
    rates = rate[0]
    gain = skip[0]

    def wide(ref, at):
        return jnp.concatenate([ref[0, at]] * repeat, axis=1)

    def narrow(x):
        return sum(x[:, i * LANES : (i + 1) * LANES] for i in range(repeat))

    def place_of(t):
        return t + falling * (length - 1 - 2 * t)

    @pl.when(pl.program_id(1) == 0)
    def _():
        inputs_back[...] = jnp.zeros_like(inputs_back)
        reads_back[...] = jnp.zeros_like(reads_back)

    held[0] = first[0]

    def forward(t, state):
        at = place_of(t)
        step = row_of(steps, at)
        act = row_of(active, at)
        state = jnp.exp(step * rates) * state + (step * act) * wide(inputs, at)
        held[t + 1] = state
        out = jnp.sum(wide(reads, at) * state, axis=0, keepdims=True)
        result[0, pl.ds(at, 1), :] = out + gain * act
        return state

    lax.fori_loop(0, length, forward, first[0], unroll=UNROLL)

    def backward(i, carry):
        adjoint, rate_sum, skip_sum = carry
        t = length - 1 - i
        at = place_of(t)
        step = row_of(steps, at)
        act = row_of(active, at)
        grad = row_of(back, at)
        adjoint = adjoint + grad * wide(reads, at)
        reads_back[0, at] += narrow(grad * held[t + 1])
        passed = jnp.exp(step * rates) * adjoint
        decay_back = passed * held[t]
        inputs_back[0, at] += narrow(adjoint * (step * act))
        drive_back = jnp.sum(adjoint * wide(inputs, at), axis=0, keepdims=True)
        steps_back[0, pl.ds(at, 1), :] = (
            jnp.sum(decay_back * rates, axis=0, keepdims=True) + act * drive_back
        )
        active_back[0, pl.ds(at, 1), :] = step * drive_back + gain * grad
        return (passed, rate_sum + decay_back * step, skip_sum + grad * act)

    start = (late[0], jnp.zeros_like(rates), jnp.zeros_like(gain))
    _, rate_sum, skip_sum = lax.fori_loop(0, length, backward, start, unroll=UNROLL)
    rate_back[0] = rate_sum * rates
    skip_back[0] = skip_sum


def specs_of(length, tile):
    rows = pl.BlockSpec((1, length, tile), lambda d, c: (d, 0, c))
    shared = pl.BlockSpec((1, length, tile), lambda d, c: (0, 0, c))
    spread = pl.BlockSpec((1, length, N, LANES), lambda d, c: (d, 0, 0, 0))
    state = pl.BlockSpec((1, N, tile), lambda d, c: (d, 0, c))
    single = pl.BlockSpec((1, 1, tile), lambda d, c: (d, 0, c))
    return (rows, shared, spread, state, single)


def summarise(active, steps, back, inputs, reads, rate):
    _, length, channels = active.shape
    tile = min(TILE, channels)
    rows, shared, spread, state, _ = specs_of(length, tile)
    return pl.pallas_call(
        summary_kernel,
        grid=(2, channels // tile),
        in_specs=[rows, rows, shared, spread, spread, state],
        out_specs=[state, state, state],
        out_shape=[jax.ShapeDtypeStruct(rate.shape, jnp.float32)] * 3,
        compiler_params=pltpu.CompilerParams(vmem_limit_bytes=LIMIT),
    )(active, steps, back, inputs, reads, rate)


def scan_all(active, steps, back, inputs, reads, rate, skip, first, late):
    _, length, channels = active.shape
    tile = min(TILE, channels)
    rows, shared, spread, state, single = specs_of(length, tile)
    full = jax.ShapeDtypeStruct(active.shape, jnp.float32)
    narrow = jax.ShapeDtypeStruct(inputs.shape, jnp.float32)
    return pl.pallas_call(
        scan_kernel,
        grid=(2, channels // tile),
        in_specs=[rows, rows, shared, spread, spread, state, single, state, state],
        out_specs=[rows, rows, rows, spread, spread, state, single],
        out_shape=[
            full, full, full, narrow, narrow,
            jax.ShapeDtypeStruct(rate.shape, jnp.float32),
            jax.ShapeDtypeStruct(skip.shape, jnp.float32),
        ],
        scratch_shapes=[pltpu.VMEM((length + 1, N, tile), jnp.float32)],
        compiler_params=pltpu.CompilerParams(vmem_limit_bytes=LIMIT),
    )(active, steps, back, inputs, reads, rate, skip, first, late)


def chain(decays, states, reverse):
    count = lax.axis_size("seq")
    place = lax.axis_index("seq")
    ahead = count - 1 - place if reverse else place
    state = jnp.zeros_like(states[0])
    for step in range(count - 1):
        source = count - 1 - step if reverse else step
        state = jnp.where(step < ahead, decays[source] * state + states[source], state)
    return state


def pack_rows(arrays, multiple):
    fw, fb, sw, tw, tb, lr, sg = arrays
    channels = fb.shape[1]
    rows = [fw, fb, sw.transpose(0, 2, 1), tw, tb, lr, sg]
    rows = [row.reshape(-1, channels) for row in rows]
    used = sum(row.shape[0] for row in rows)
    pad = -used % multiple
    return jnp.concatenate(rows + [jnp.zeros((pad, channels), jnp.float32)], axis=0)


def unpack_rows(packed):
    channels = packed.shape[1]
    sizes = (2 * K, 2, 2 * (R + 2 * N), 2 * R, 2, 2 * N, 2)
    parts = []
    start = 0
    for size in sizes:
        parts.append(packed[start : start + size])
        start += size
    return (
        parts[0].reshape(2, K, channels),
        parts[1],
        parts[2].reshape(2, R + 2 * N, channels).transpose(0, 2, 1),
        parts[3].reshape(2, R, channels),
        parts[4],
        parts[5].reshape(2, N, channels),
        parts[6],
    )


def spread_rows(block):
    share = block.shape[0] // lax.axis_size("seq")
    part = lax.dynamic_slice_in_dim(block, lax.axis_index("seq") * share, share, axis=0)
    part = lax.all_gather(part, "dp", axis=0)
    parts = lax.all_gather(part, "seq", axis=0)
    return parts.transpose(1, 0, 2, 3).reshape(parts.shape[1], -1, block.shape[1])


def shards(
    tokens,
    cotangent,
    input_weight,
    filter_weight,
    filter_bias,
    scan_weight,
    step_weight,
    step_bias,
    log_rate,
    skip_gain,
):
    full_weight = spread_rows(input_weight)
    full_weight = full_weight.reshape(-1, input_weight.shape[1])
    packed = pack_rows(
        (filter_weight, filter_bias, scan_weight, step_weight, step_bias, log_rate, skip_gain), 128
    )
    spread = spread_rows(packed)
    params = unpack_rows(spread.transpose(1, 0, 2).reshape(packed.shape[0], -1))
    all_tokens = lax.all_gather(tokens[0], "seq", axis=0, tiled=True)
    inputs = tokens[0]
    projected = jnp.dot(inputs, full_weight, preferred_element_type=jnp.float32).astype(
        jnp.bfloat16
    )
    width = projected.shape[1] // 2
    rim = K - 1
    widened = extended(projected[:, :width], (("seq", 0),), rim)
    padded = widened.astype(jnp.float32)
    gates = projected[:, width:].astype(jnp.float32)
    prepared_list = []
    prep_pulls = []
    for which in range(2):
        prepared, prep_pull = jax.vjp(
            partial(prepare, which=which),
            padded,
            params[0],
            params[1],
            params[2],
            params[3],
            params[4],
        )
        prepared_list.append(prepared)
        prep_pulls.append(prep_pull)
    gate, gate_pull = jax.vjp(jax.nn.silu, gates)
    tangent = cotangent[0].astype(jnp.float32)
    back_total = tangent * gate
    active, steps, inputs_coef, reads = (jnp.stack(pair) for pair in zip(*prepared_list))
    inputs_wide = jnp.broadcast_to(inputs_coef[..., None], inputs_coef.shape + (LANES,))
    reads_wide = jnp.broadcast_to(reads[..., None], reads.shape + (LANES,))
    rate = -jnp.exp(params[5])
    operands = (active, steps, back_total[None], inputs_wide, reads_wide, rate)
    states, flows, decays = summarise(*operands)
    told = lax.all_gather(jnp.concatenate([states, flows, decays]), "seq", axis=0)
    first = jnp.stack(
        [chain(told[:, 4], told[:, 0], False), chain(told[:, 5], told[:, 1], True)]
    )
    late = jnp.stack(
        [chain(told[:, 4], told[:, 2], True), chain(told[:, 5], told[:, 3], False)]
    )
    results = scan_all(*operands, params[6][:, None], first, late)
    outputs, active_back, steps_back, inputs_back, reads_back, rates_back, skip_back = results
    inputs_back = jnp.sum(inputs_back, axis=-1)
    reads_back = jnp.sum(reads_back, axis=-1)
    skip_back = skip_back[:, 0]
    total = outputs[0] + outputs[1]
    mixed = (total * gate).astype(jnp.bfloat16)
    back_gates = gate_pull(tangent * total)[0]
    back_padded = jnp.zeros_like(padded)
    param_backs = [jnp.zeros_like(param) for param in params[:5]]
    for which in range(2):
        more = prep_pulls[which](
            (active_back[which], steps_back[which], inputs_back[which], reads_back[which])
        )
        back_padded = back_padded + more[0]
        param_backs = [older + newer for older, newer in zip(param_backs, more[1:])]
    rims = jnp.concatenate([back_padded[:rim], back_padded[-rim:]], axis=0)
    returned = extended(rims, (("seq", 0),), rim)
    middle = back_padded[rim:-rim]
    back_values = jnp.concatenate(
        [middle[:rim] + returned[:rim], middle[rim:-rim], middle[-rim:] + returned[-rim:]], axis=0
    )
    back_projected = jnp.concatenate([back_values, back_gates], axis=1).astype(jnp.bfloat16)
    tokens_back = lax.dot_general(
        back_projected, full_weight, (((1,), (1,)), ((), ())), preferred_element_type=jnp.float32
    ).astype(jnp.bfloat16)
    groups, peers = lax.axis_size("dp"), lax.axis_size("seq")
    all_back = lax.all_gather(back_projected, "seq", axis=0, tiled=True)
    depth = all_tokens.shape[1]
    shared = all_tokens.reshape(all_tokens.shape[0], groups, peers, depth // (groups * peers))
    mine = lax.dynamic_index_in_dim(shared, lax.axis_index("seq"), 2, False)
    weight_back = lax.dot_general(
        mine.reshape(mine.shape[0], -1),
        all_back,
        (((0,), (0,)), ((), ())),
        preferred_element_type=jnp.float32,
    ).astype(jnp.bfloat16)
    wide = weight_back.shape[1]
    weight_back = weight_back.reshape(groups, -1, wide)
    own = skip_back.shape[1] // (groups * peers)
    small = pack_rows((*param_backs, rates_back, skip_back), wide // own).astype(jnp.bfloat16)
    height = small.shape[0]
    small = small.reshape(height, groups, peers, own).transpose(2, 1, 0, 3)
    small = lax.all_to_all(small.reshape(peers, groups, -1, wide), "seq", 0, 0)
    small = jnp.sum(small.astype(jnp.float32), axis=0).astype(jnp.bfloat16)
    joined = jnp.concatenate([weight_back, small], axis=1)
    joined = lax.all_to_all(joined, "dp", 0, 0)
    joined = jnp.sum(joined.astype(jnp.float32), axis=0)
    edge = weight_back.shape[1]
    sums = (joined[:edge], *unpack_rows(joined[edge:].reshape(height, own)))
    return (
        mixed[None],
        tokens_back[None],
        sums[0],
        sums[1],
        sums[2],
        sums[3],
        sums[4],
        sums[5],
        sums[6],
        sums[7],
    )


def solution(mesh):
    in_specs = (
        P("dp", "seq", None),
        P("dp", "seq", None),
        P("dp", None),
        P(None, None, "dp"),
        P(None, "dp"),
        P(None, "dp", None),
        P(None, None, "dp"),
        P(None, "dp"),
        P(None, None, "dp"),
        P(None, "dp"),
    )
    out_specs = (
        P("dp", "seq", None),
        P("dp", "seq", None),
        P(("dp", "seq"), None),
        P(None, None, ("dp", "seq")),
        P(None, ("dp", "seq")),
        P(None, ("dp", "seq"), None),
        P(None, None, ("dp", "seq")),
        P(None, ("dp", "seq")),
        P(None, None, ("dp", "seq")),
        P(None, ("dp", "seq")),
    )
    return jax.shard_map(shards, mesh=mesh, in_specs=in_specs, out_specs=out_specs, check_vma=False)
```

time: 1350 us -> 481 us (0.36); the launches traced: 1330 us -> 476 us
  local copies, waits for them, and re-layouts: 408 us -> 71.9 us
  other arithmetic: 303 us -> 26.7 us
  matrix products: 280 us -> 36.7 us
  waiting for transfers between devices: 292 us -> 191 us
  Pallas kernels: 0 us -> 76 us
  blocking collectives: 0 us -> 37.1 us
    dot_general x576 -> x0, matrix products: 245 us -> none  [the longest x512 149 us: block_advance(): results.append(jnp.dot(read_part[place], state, precision=HIGH))]
    squeeze x320 -> x0, local copies, waits for them, and re-layouts: 151 us -> none  [the longest x256 121 us: forward_summary(): (state, elapsed), _ = lax.scan(forward_advance, start, blocks)]
    all_gather x4, waiting for transfers between devices: 219 us -> 118 us  [the longest x2 74.9 us: spread_rows(): parts = lax.all_gather(part, 'seq', axis=0)]
    dynamic_update_slice x160 -> x0, other arithmetic: 95.9 us -> none  [block_scan(): lax.scan(jax.checkpoint(block_advance), state_in, blocks)]
    pallas_call x0 -> x2, Pallas kernels: none -> 76 us  [the longest x1 56 us: scan_all(): pl.pallas_call(scan_kernel, grid=(2, channels // tile), in_specs=[rows, r...]
    mul x160 -> x0, other arithmetic: 67.3 us -> none  [the longest x32 28.6 us: forward_advance(): step_part * active_part]
    reduce_sum x162 -> x2, other arithmetic: 58.4 us -> 4.45 us  [the longest x1 2.23 us: shards(): inputs_back = jnp.sum(inputs_back, axis=-1)]
    slice x197 -> x3, local copies, waits for them, and re-layouts: 47.9 us -> 0.65 us  [the longest x1 0.63 us: prepare(): step_bias[which]]
  transfers between devices with their start and end apart: 12 -> 12, of which waited for: 7 -> 8; matrix products, arithmetic and copies ran while one was open for 34% -> 19% of each run, Pallas kernels for 0% -> 12%
where the time goes in v2:
time: 481 us; the launch traced here: 476 us
  waiting for transfers between devices  191 us (40%)
  Pallas kernels  76 us (16%)
  local copies, waits for them, and re-layouts  71.9 us (15%)
  blocking collectives  37.1 us (8%)
  matrix products  36.7 us (8%)
  other arithmetic  26.7 us (6%)
  starting transfers between devices  19.9 us (4%)
  between operations  16 us (3%)
    all_gather x2, waiting for transfers between devices, spread_rows(): parts = lax.all_gather(part, 'seq', axis=0)  74.9 us
    pallas_call x1, Pallas kernels, scan_all(): pl.pallas_call(scan_kernel, grid=(2, channels // tile), in_specs=[rows, r...  56 us
    all_to_all x1, waiting for transfers between devices, shards(): joined = lax.all_to_all(joined, 'dp', 0, 0)  51.9 us
    all_gather x1, blocking collectives, spread_rows(): part = lax.all_gather(part, 'dp', axis=0)  37.1 us
    all_gather x1, waiting for transfers between devices, shards(): lax.all_gather(jnp.concatenate([states, flows, decays]), 'seq', axis=0)  28.7 us
    pallas_call x1, Pallas kernels, summarise(): pl.pallas_call(summary_kernel, grid=(2, channels // tile), in_specs=[rows...  20 us
    all_to_all x1, waiting for transfers between devices, shards(): small = lax.all_to_all(small.reshape(peers, groups, -1, wide), 'seq', 0, 0)  19.1 us
    concatenate x11, local copies, waits for them, and re-layouts, pack_rows(): jnp.concatenate(rows + [jnp.zeros((pad, channels), jnp.float32)], axis=0)  19.1 us
  transfers between devices with their start and end apart: 12, of which 8 were waited for; matrix products, arithmetic and copies ran while one was open for 19% of the time, Pallas kernels for 12%

profile of v2, /device:TPU:0, one launch (start us, length us, event | category | flops | bytes accessed | tf_op | source)
XLA Modules:
  0.0 475.6 jit_solution(10700412660597625302)
XLA Ops:
  9.9 5.0 %concatenate.39 = f32[384,256]{1,0:T(8,128)S(1)} concatenate(f32[8,256]{1,0:T(8,128)S(1)} %reshape.528, f32[2,256]{1,0:T(2,128)} %param.15, f32[192,256]{1,0:T(8,128)} %bitcast.281, f32[128,256]{1,0:T(8,128)} %bitcast.282, f32[2,256]{1,0:T(2,128)} %param.18, f32[32,256]{1,0:T(8,128)} %bitcast.290, f32[2,256]{1,0:T(2,128)} %param.20, f32[18,256]{1,0:T(8,128)S(1)} %broadcast_in_dim.70), dimensions={0} | concatenate | bytes 786432 | tf_op jit(solution)/shard_map/concatenate | solution.py:210
  14.9 37.1 %all-gather = f32[768,256]{1,0:T(8,128)} all-gather(f32[96,256]{1,0:T(8,128)S(1)} %constant_dynamic-slice_fusion.2), channel_id=2, replica_groups=mesh['dp'=8,'seq'=4] {'dp'}, dimensions={0}, use_global_device_ids=true | all-gather | bytes 884736 | tf_op jit(solution)/shard_map/all_gather | solution.py:235
  52.1 14.8 %all-gather.17.cloned.1.call-done = bf16[256,4096]{1,0:T(8,128)(2,1)} async-done(((bf16[32,4096]{1,0:T(8,128)(2,1)}), bf16[256,4096]{1,0:T(8,128)(2,1)}) %all-gather.17.cloned.1.call-update) | async-done | bytes 2097168 | tf_op jit(solution)/shard_map/all_gather | solution.py:235
  67.0 29.4 %all-gather.15.cloned.1.call-done = f32[32,96,256]{2,1,0:T(8,128)} async-done(((f32[8,96,256]{2,1,0:T(8,128)}), f32[32,96,256]{2,1,0:T(8,128)}) %all-gather.15.cloned.1.call-update) | async-done | bytes 3145744 | tf_op jit(solution)/shard_map/all_gather | solution.py:236
  100.0 3.6 copy.96
  103.6 2.7 reshape.534
  110.8 45.5 %all-gather.19.cloned.1.call-done = bf16[32,32,4096]{2,1,0:T(8,128)(2,1)} async-done(((bf16[8,32,4096]{2,1,0:T(8,128)(2,1)}), bf16[32,32,4096]{2,1,0:T(8,128)(2,1)}) %all-gather.19.cloned.1.call-update) | async-done | bytes 8388624 | tf_op jit(solution)/shard_map/all_gather | solution.py:236
  156.3 7.8 %copy.95 = bf16[8,4,32,4096]{3,2,1,0:T(8,128)(2,1)} copy(bf16[8,4,32,4096]{3,2,0,1:T(8,128)(2,1)} %bitcast.260) | data formatting | bytes 16777216 | tf_op jit(solution)/shard_map/transpose | solution.py:237
  164.1 4.7 fusion
  174.4 2.6 fusion.66
  192.5 20.0 %shard_map.177 = (f32[2,16,2048]{2,1,0:T(8,128)S(1)}, f32[2,16,2048]{2,1,0:T(8,128)S(1)}, f32[2,16,2048]{2,1,0:T(8,128)S(1)}) custom-call(f32[2,128,2048]{2,1,0:T(8,128)S(1)} %pad_maximum_fusion.1.active, f32[2,128,2048]{2,1,0:T(8,128)} %pad_maximum_fusion.2.steps, f32[1,128,2048]{2,1,0:T(8,128)S(1)} %fusion.2.back, ...), custom_call_target="tpu_custom_call" | custom-call | tf_op jit(solution)/shard_map/pallas_call | solution.py:161
  215.6 28.7 %all-gather.21.cloned.1.call-done = f32[24,16,2048]{2,1,0:T(8,128)} async-done(((f32[6,16,2048]{2,1,0:T(8,128)}), f32[24,16,2048]{2,1,0:T(8,128)}) %all-gather.21.cloned.1.call-update) | async-done | bytes 3145744 | tf_op jit(solution)/shard_map/all_gather | solution.py:292
  247.4 56.0 %shard_map.178 = (f32[2,128,2048]{2,1,0:T(8,128)S(1)}, f32[2,128,2048]{2,1,0:T(8,128)}, f32[2,128,2048]{2,1,0:T(8,128)}, f32[2,128,16,128]{3,2,1,0:T(8,128)}, f3...) custom-call(f32[2,128,2048]{2,1,0:T(8,128)} %copy-done.2, ...), custom_call_target="tpu_custom_call" | custom-call | tf_op jit(solution)/shard_map/pallas_call | solution.py:177
  303.4 3.4 fusion.70
  309.0 2.2 reduce_sum.146
  311.3 2.2 reduce_sum.147
  313.6 2.3 fusion.81
  316.1 3.3 fusion.12
  319.7 3.6 multiply_reduce_fusion.7
  327.3 3.3 collective-permute-start.2
  337.1 2.4 convolution_bitcast_fusion.1
  348.4 7.2 %concatenate.51 = bf16[384,8,4,64]{0,3,2,1:T(8,128)(2,1)} concatenate(bf16[8,8,4,64]{0,3,2,1:T(8,128)(2,1)S(1)} %copy.110, bf16[2,8,4,64]{0,3,2,1:T(8,128)(2,1)S(1)} %bitcast.271, bf16[192,8,4,64]{0,3,2,1:T(8,128)(2,1)S(1)} %concatenate.46, bf16[128,8,4,64]{0,3,2,1:T(8,128)(2,1)S(1)} %copy.112, bf16[2,8,4,64]{0,3,2,1:T(8,128)(2,1)S(1)} %bitcast.270, ...), dimensions={0} | concatenate | bytes 3145728 | tf_op jit(solution)/shard_map/concatenate | solution.py:210
  355.5 3.1 copy.115
  358.6 3.7 reshape.542
  362.3 3.6 copy.116
  365.9 5.1 %all-to-all-start = ((bf16[4,8,6,4096]{3,1,2,0:T(8,128)(2,1)}), bf16[4,8,6,4096]{3,1,2,0:T(8,128)(2,1)S(1)}, u32[]{:S(2)}, u32[]{:S(2)}) async-start(bf16[4,8,6,4096]{3,1,2,0:T(8,128)(2,1)} %copy.116), calls=%async_computation | async-start | bytes 3145728 | tf_op jit(solution)/shard_map/all_to_all | solution.py:342
  372.0 19.1 %all-to-all-done = bf16[4,8,6,4096]{3,1,2,0:T(8,128)(2,1)S(1)} async-done(((bf16[4,8,6,4096]{3,1,2,0:T(8,128)(2,1)}), bf16[4,8,6,4096]{3,1,2,0:T(8,128)(2,1)S(1)}, u32[]{:S(2)}, u32[]{:S(2)}) %all-to-all-start) | async-done | bytes 1572896 | tf_op jit(solution)/shard_map/all_to_all | solution.py:342
  391.7 3.4 convolution_convert_fusion
  397.0 6.0 %all-to-all-start.1 = ((bf16[8,38,4096]{2,1,0:T(8,128)(2,1)}), bf16[8,38,4096]{2,1,0:T(8,128)(2,1)}, u32[]{:S(2)}, u32[]{:S(2)}) async-start(bf16[8,38,4096]{2,1,0:T(8,128)(2,1)} %pad_maximum_fusion), calls=%async_computation.1 | async-start | bytes 5242880 | tf_op jit(solution)/shard_map/all_to_all | solution.py:345
  403.0 7.1 %fusion.1 = bf16[1,128,1024]{2,1,0:T(8,128)(2,1)} fusion(bf16[128,4096]{1,0:T(8,128)(2,1)S(1)} %copy-done.8, bf16[1024,4096]{1,0:T(8,128)(2,1)} %bitcast.253), kind=kOutput, calls=%fused_computation.31 | convolution fusion | flops 1073872896 | bytes 9699328 | tf_op jit(solution)/shard_map/dot_general | solution.py:322
  410.0 51.9 %all-to-all-done.1 = bf16[8,38,4096]{2,1,0:T(8,128)(2,1)} async-done(((bf16[8,38,4096]{2,1,0:T(8,128)(2,1)}), bf16[8,38,4096]{2,1,0:T(8,128)(2,1)}, u32[]{:S(2)}, u32[]{:S(2)}) %all-to-all-start.1) | async-done | bytes 2490400 | tf_op jit(solution)/shard_map/all_to_all | solution.py:345
  462.0 2.2 convert_reduce_fusion
  (257 shorter events, 66.7 us)
Async XLA Ops:
  7.2 59.7 %all-gather.17.cloned.1.call-start = ((), (), s32[]{:S(2)}) async-start(), calls=%async_computation.4 | async-start | bytes 2359296 | tf_op jit(solution)/shard_map/all_gather | solution.py:235
  9.2 87.2 %all-gather.15.cloned.1.call-start = ((), (), s32[]{:S(2)}) async-start(), calls=%async_computation.3 | async-start | bytes 3932160 | tf_op jit(solution)/shard_map/all_gather | solution.py:236
  52.0 104.3 %all-gather.19.cloned.1.call-start = ((), (), s32[]{:S(2)}) async-start(), calls=%async_computation.5 | async-start | bytes 10485760 | tf_op jit(solution)/shard_map/all_gather | solution.py:236
  66.9 177.3 %all-gather.21.cloned.1.call-start = ((), (), s32[]{:S(2)}) async-start(), calls=%async_computation.6 | async-start | bytes 3932160 | tf_op jit(solution)/shard_map/all_gather | solution.py:292
  98.5 11.5 %copy-start.7 = (f32[8,4,96,256]{3,2,1,0:T(8,128)}, f32[8,4,96,256]{3,2,1,0:T(8,128)S(1)}, u32[]{:S(2)}) copy-start(f32[8,4,96,256]{3,2,1,0:T(8,128)S(1)} %copy.93) | copy-start | bytes 9437188
  110.7 63.6 %copy-start.40 = (f32[1,1,2048]{2,1,0:T(1,128)}, f32[1,1,2048]{2,1,0:T(1,128)S(1)}, u32[]{:S(2)}) copy-start(f32[1,1,2048]{2,1,0:T(1,128)S(1)} %get-tuple-element.93) | copy-start | bytes 24580
  110.7 63.6 %copy-start.42 = (f32[1,1,2048]{2,1,0:T(1,128)}, f32[1,1,2048]{2,1,0:T(1,128)S(1)}, u32[]{:S(2)}) copy-start(f32[1,1,2048]{2,1,0:T(1,128)S(1)} %get-tuple-element.94) | copy-start | bytes 24580
  110.7 63.6 %copy-start.44 = (f32[1,1,2048]{2,1,0:T(1,128)}, f32[1,1,2048]{2,1,0:T(1,128)S(1)}, u32[]{:S(2)}) copy-start(f32[1,1,2048]{2,1,0:T(1,128)S(1)} %get-tuple-element.95) | copy-start | bytes 24580
  110.7 63.6 %copy-start.46 = (f32[1,1,2048]{2,1,0:T(1,128)}, f32[1,1,2048]{2,1,0:T(1,128)S(1)}, u32[]{:S(2)}) copy-start(f32[1,1,2048]{2,1,0:T(1,128)S(1)} %get-tuple-element.96) | copy-start | bytes 24580
  110.7 63.6 %copy-start.48 = (f32[1,1,2048]{2,1,0:T(1,128)}, f32[1,1,2048]{2,1,0:T(1,128)S(1)}, u32[]{:S(2)}) copy-start(f32[1,1,2048]{2,1,0:T(1,128)S(1)} %get-tuple-element.97) | copy-start | bytes 24580
  110.7 63.6 %copy-start.50 = (f32[1,1,2048]{2,1,0:T(1,128)}, f32[1,1,2048]{2,1,0:T(1,128)S(1)}, u32[]{:S(2)}) copy-start(f32[1,1,2048]{2,1,0:T(1,128)S(1)} %get-tuple-element.98) | copy-start | bytes 24580
  110.7 63.6 %copy-start.52 = (f32[1,1,2048]{2,1,0:T(1,128)}, f32[1,1,2048]{2,1,0:T(1,128)S(1)}, u32[]{:S(2)}) copy-start(f32[1,1,2048]{2,1,0:T(1,128)S(1)} %get-tuple-element.99) | copy-start | bytes 24580
  110.8 63.6 %copy-start.54 = (f32[1,1,2048]{2,1,0:T(1,128)}, f32[1,1,2048]{2,1,0:T(1,128)S(1)}, u32[]{:S(2)}) copy-start(f32[1,1,2048]{2,1,0:T(1,128)S(1)} %get-tuple-element.100) | copy-start | bytes 24580
  156.3 7.8 %copy-start.27 = (bf16[1,128,1024]{2,1,0:T(8,128)(2,1)S(1)}, bf16[1,128,1024]{2,1,0:T(8,128)(2,1)}, u32[]{:S(2)}) copy-start(bf16[1,128,1024]{2,1,0:T(8,128)(2,1)} %param.11) | copy-start | bytes 786436
  164.1 8.4 %copy-start.25 = (bf16[1,128,2048]{2,1,0:T(8,128)(2,1)S(1)}, bf16[1,128,2048]{2,1,0:T(8,128)(2,1)}, u32[]{:S(2)}) copy-start(bf16[1,128,2048]{2,1,0:T(8,128)(2,1)} %param.12) | copy-start | bytes 1572868
  168.8 5.5 %copy-start.17 = (bf16[128,4096]{1,0:T(8,128)(2,1)}, bf16[128,4096]{1,0:T(8,128)(2,1)S(1)}, u32[]{:S(2)}) copy-start(bf16[128,4096]{1,0:T(8,128)(2,1)S(1)} %fusion) | copy-start | bytes 3145732
  168.9 4.0 collective-permute-start
  171.1 3.1 collective-permute-start.1
  188.6 4.0 copy-start.2
  213.5 157.5 %all-gather.23.cloned.1.call-start = ((), (), s32[]{:S(2)}) async-start(), calls=%async_computation.7 | async-start | bytes 1310720 | tf_op jit(solution)/shard_map/all_gather | solution.py:259
  214.4 177.2 %all-gather.13.cloned.1.call-start = ((), (), s32[]{:S(2)}) async-start(), calls=%async_computation.2 | async-start | bytes 5242880 | tf_op jit(solution)/shard_map/all_gather | solution.py:326
  247.4 56.0 %copy-start.14 = (f32[128,2048]{1,0:T(8,128)S(1)}, f32[128,2048]{1,0:T(8,128)}, u32[]{:S(2)}) copy-start(f32[128,2048]{1,0:T(8,128)} %copy-done.13) | copy-start | bytes 3145732
  247.4 56.0 %copy-start.16 = (f32[128,2048]{1,0:T(8,128)S(1)}, f32[128,2048]{1,0:T(8,128)}, u32[]{:S(2)}) copy-start(f32[128,2048]{1,0:T(8,128)} %copy-done.15) | copy-start | bytes 3145732
  303.4 4.4 copy-start.21
  306.8 6.8 %copy-start.9 = (f32[128,2048]{1,0:T(8,128)}, f32[128,2048]{1,0:T(8,128)S(1)}, u32[]{:S(2)}) copy-start(f32[128,2048]{1,0:T(8,128)S(1)} %get-tuple-element.73) | copy-start | bytes 3145732
  323.3 7.3 %collective-permute-start.3 = (f32[3,2048]{1,0:T(4,128)S(1)}, f32[3,2048]{1,0:T(4,128)S(1)}, u32[]{:S(2)}, u32[]{:S(2)}) collective-permute-start(f32[3,2048]{1,0:T(4,128)S(1)} %add_add_fusion.1), channel_id=1, source_target_pairs={{1,0},{2,1},{3,2},{5,4},{6,5},{7,6},{9,8},{10,9},{11,10},{13,12},{... | collective-permute-start | bytes 73736 | tf_op jit(solution)/shard_map/ppermute | solution.py:26
  327.3 3.9 collective-permute-start.2
  342.3 6.0 %copy-start.24 = (bf16[2,2048]{0,1:T(8,128)(2,1)S(1)}, bf16[2,2048]{0,1:T(8,128)(2,1)}, u32[]{:S(2)}) copy-start(bf16[2,2048]{0,1:T(8,128)(2,1)} %copy.109) | copy-start | bytes 24580
  365.9 25.2 %all-to-all-start = ((bf16[4,8,6,4096]{3,1,2,0:T(8,128)(2,1)}), bf16[4,8,6,4096]{3,1,2,0:T(8,128)(2,1)S(1)}, u32[]{:S(2)}, u32[]{:S(2)}) async-start(bf16[4,8,6,4096]{3,1,2,0:T(8,128)(2,1)} %copy.116), calls=%async_computation | async-start | bytes 3145728 | tf_op jit(solution)/shard_map/all_to_all | solution.py:342
  397.0 6.0 %copy-start.8 = (bf16[128,4096]{1,0:T(8,128)(2,1)S(1)}, bf16[128,4096]{1,0:T(8,128)(2,1)}, u32[]{:S(2)}) copy-start(bf16[128,4096]{1,0:T(8,128)(2,1)} %pad_maximum_fusion.3) | copy-start | bytes 3145732
  397.0 65.0 %all-to-all-start.1 = ((bf16[8,38,4096]{2,1,0:T(8,128)(2,1)}), bf16[8,38,4096]{2,1,0:T(8,128)(2,1)}, u32[]{:S(2)}, u32[]{:S(2)}) async-start(bf16[8,38,4096]{2,1,0:T(8,128)(2,1)} %pad_maximum_fusion), calls=%async_computation.1 | async-start | bytes 5242880 | tf_op jit(solution)/shard_map/all_to_all | solution.py:345
  402.9 65.3 %copy-start.1 = (bf16[128,4096]{1,0:T(8,128)(2,1)S(1)}, bf16[128,4096]{1,0:T(8,128)(2,1)}, u32[]{:S(2)}) copy-start(bf16[128,4096]{1,0:T(8,128)(2,1)} %param.13) | copy-start | bytes 3145732
  (51 other events, 121.5 us)
Sparse Core Ops, SparseCore 0:
  10.7 56.1 all-gather.16
  68.5 27.8 all-gather.14
  98.0 58.2 all-gather.18
  213.7 30.5 all-gather.20
  245.7 16.8 all-gather.22
  332.5 37.7 all-gather.12
